TPU v7x, 256 devices: a whole 4x4x8 slice. The times are simulated.
256 devices in a mesh: prefix: 32 (over x, y, core), req: 8 (over z).
Axes of the slice: x: 4, y: 4, z: 8, core: 2. Of those that a mesh axis runs over, the one named last changes fastest.
Arguments:
- queries: bfloat16 [512, 8192], P(('prefix', 'req')), may hold values from -32 to 32
- prefix_keys: bfloat16 [131072, 1024], P('prefix', 'req'), may hold values from -15 to 15
- prefix_values: bfloat16 [131072, 1024], P('prefix', 'req'), may hold values from -16 to 16
- suffix_keys: bfloat16 [512, 1024, 1024], P(('prefix', 'req')), may hold values from -4 to 4
- suffix_values: bfloat16 [512, 1024, 1024], P(('prefix', 'req')), may hold values from -16 to 16
- suffix_lengths: int32 [512], P(('prefix', 'req')), may hold values from 256 to 1024, as said below
Outputs:
- attended: float32 [512, 8192], P(('prefix', 'req'))
Inputs may be any that keep to these rules, and one draw needn't show every extreme that they name: `suffix_lengths`: some request has exactly 1024 live positions.
All inputs are finite; a program needn't handle non-finite values.
Results may differ from a plain program's by a relative error of at most 0.0045.
Values may be sent and summed in bfloat16 or wider, within the bound.
A program may use at most 128 MiB of HBM per device.

v0:
```python
import math

import jax
import jax.numpy as jnp
from jax import lax
from jax.sharding import PartitionSpec as P

HEADS = 64
KVH = 8
HD = 128


def join_parts(former, latter):
    mass_a, out_a = former
    mass_b, out_b = latter
    width_each = out_a.shape[1] // mass_a.shape[1]
    joined = jnp.logaddexp(mass_a, mass_b)
    left_share = jnp.repeat(jnp.exp(mass_a - joined), width_each, axis=1)
    right_share = jnp.repeat(jnp.exp(mass_b - joined), width_each, axis=1)
    return (joined, out_a * left_share + out_b * right_share)


def local(queries, prefix_keys, prefix_values, suffix_keys, suffix_values, suffix_lengths):
    rows_own, width = queries.shape
    n_prefix = lax.axis_size("prefix")
    per_group = HEADS // KVH
    kv_local = prefix_keys.shape[1] // HD
    score_scale = 1.0 / math.sqrt(HD)
    routed = lax.all_to_all(queries, "req", split_axis=1, concat_axis=0, tiled=True)
    gathered = lax.all_gather(routed, "prefix", axis=0, tiled=True)
    own_heads = queries.reshape(rows_own, KVH, per_group, HD)
    suffix_k = suffix_keys.reshape(rows_own, -1, KVH, HD)
    suffix_v = suffix_values.reshape(rows_own, -1, KVH, HD)
    positions = suffix_k.shape[1]
    live = suffix_lengths[:, None, None, None]
    all_scores = (
        jnp.einsum("bjgd,bsjd->bjgs", own_heads, suffix_k, preferred_element_type=jnp.float32)
        * score_scale
    )
    in_range = lax.broadcasted_iota(jnp.int32, (rows_own, 1, 1, positions), 3) < live
    all_scores = jnp.where(in_range, all_scores, -jnp.inf)
    row_top = jnp.max(all_scores, axis=-1)
    weights = jnp.exp(all_scores - row_top[..., None])
    row_total = jnp.sum(weights, axis=-1)
    summed = jnp.einsum(
        "bjgs,bsjd->bjgd",
        weights.astype(jnp.bfloat16),
        suffix_v,
        preferred_element_type=jnp.float32,
    )
    suffix_mass = (row_top + jnp.log(row_total)).reshape(rows_own, HEADS)
    suffix_out = (summed / row_total[..., None]).reshape(rows_own, HEADS * HD)
    total_rows = gathered.shape[0]
    row_block = math.gcd(total_rows, 64)
    query_blocks = gathered.reshape(total_rows // row_block, row_block, kv_local, per_group, HD)
    keys_local = prefix_keys.reshape(-1, kv_local, HD)
    values_local = prefix_values.reshape(-1, kv_local, HD)

    def prefix_block(query_block):
        block_scores = (
            jnp.einsum(
                "bjgd,njd->bjgn", query_block, keys_local, preferred_element_type=jnp.float32
            )
            * score_scale
        )
        block_top = jnp.max(block_scores, axis=-1)
        weights = jnp.exp(block_scores - block_top[..., None])
        block_total = jnp.sum(weights, axis=-1)
        block_sum = jnp.einsum(
            "bjgn,njd->bjgd",
            weights.astype(jnp.bfloat16),
            values_local,
            preferred_element_type=jnp.float32,
        )
        block_mass = block_top + jnp.log(block_total)
        block_out = block_sum / block_total[..., None]
        return (block_mass.reshape(row_block, -1), block_out.reshape(row_block, -1))

    log_mass, partial_out = lax.map(prefix_block, query_blocks)
    log_mass = log_mass.reshape(total_rows, -1)
    partial_out = partial_out.reshape(total_rows, -1)
    heads_local = log_mass.shape[1]
    rows_mine = total_rows // n_prefix
    mass_in, part_in = (
        lax.all_to_all(log_mass, "prefix", split_axis=0, concat_axis=0, tiled=True),
        lax.all_to_all(partial_out, "prefix", split_axis=0, concat_axis=0, tiled=True),
    )
    mass_in = mass_in.reshape(n_prefix, rows_mine, heads_local)
    part_in = part_in.reshape(n_prefix, rows_mine, heads_local, HD)
    mass_top = jnp.max(mass_in, axis=0)
    mine_mass = mass_top + jnp.log(jnp.sum(jnp.exp(mass_in - mass_top[None]), axis=0))
    shares = jnp.exp(mass_in - mine_mass[None])
    mine_out = jnp.sum(part_in * shares[..., None], axis=0).reshape(rows_mine, heads_local * HD)
    back_mass, back_out = (
        lax.all_to_all(mine_mass, "req", split_axis=0, concat_axis=1, tiled=True),
        lax.all_to_all(mine_out, "req", split_axis=0, concat_axis=1, tiled=True),
    )
    final_mass, final_out = join_parts((back_mass, back_out), (suffix_mass, suffix_out))
    return final_out


def solution(mesh):
    return jax.shard_map(
        local,
        mesh=mesh,
        in_specs=(
            P(("prefix", "req"), None),
            P("prefix", "req"),
            P("prefix", "req"),
            P(("prefix", "req"), None, None),
            P(("prefix", "req"), None, None),
            P(("prefix", "req")),
        ),
        out_specs=P(("prefix", "req"), None),
        check_vma=False,
    )
```

profile of v0, /device:TPU:8, one launch (start us, length us, event | category | flops | bytes accessed | tf_op | source)
XLA Modules:
  0.0 201.5 jit_solution(18085518708224357755)
XLA Ops:
  6.5 16.5 %all_to_all.72 = bf16[2,8,1024]{2,0,1:T(2,128)(2,1)S(1)} all-to-all(bf16[2,8,1024]{2,0,1:T(2,128)(2,1)} %bitcast.160), channel_id=1, replica_groups=mesh['prefix'=32,'req'=8] {'req'}, dimensions={1} | all-to-all | bytes 65536 | tf_op jit(solution)/shard_map/all_to_all | solution.py:29
  23.0 0.6 all_to_all.55
  23.7 0.0 all-gather.2.cloned.1.call-update
  23.7 43.8 %all-gather.2.cloned.1.call-done = bf16[512,1024]{1,0:T(8,128)(2,1)} async-done(((bf16[16,1024]{1,0:T(8,128)(2,1)}), bf16[512,1024]{1,0:T(8,128)(2,1)}) %all-gather.2.cloned.1.call-update) | async-done | bytes 1048592 | tf_op jit(solution)/shard_map/all_gather | solution.py:30
  67.5 1.5 copy.40
  69.0 50.4 %while.12 = (s32[]{:T(128)}, f32[8,64,8]{2,1,0:T(8,128)S(1)}, f32[8,64,1024]{2,1,0:T(8,128)}, bf16[8,64,1,8,128]{4,3,1,2,0:T(8,128)(2,1)S(1)}, bf16[4096,1,128]{...) while((s32[]{:T(128)}, f32[8,64,8]{2,1,0:T(8,128)S(1)}, f32[8,64,1024]{2,1,0:T(8,128)}, ...), condition=%wide.region_3.4_spmd, body=%wide.region_0.3_spmd.sunk | while | flops 1090584064 | bytes 33008240 | solution.py:79
  69.0 2.6 %bitcast_reduce_fusion.3 = (f32[64,8]{1,0:T(8,128)S(1)}, f32[64,8,4096]{2,1,0:T(8,128)S(1)}) fusion(bf16[4096,1,128]{2,0,1:T(8,128)(2,1)} %get-tuple-element.119, bf16[8,64,1,8,128]{4,3,1,2,0:T(8,128)(2,1)S(1)} %get-tuple-element.118, s32[]{:T(128)} %get-tuple-element.108), kind=kOutput, calls=%fused_computation.1.clone.1 | convolution fusion | flops 541064704 | bytes 9570308 | tf_op jit(solution)/shard_map/while/body/eval_jaxpr/bjgd,njd->bjgn/dot_general | solution.py:61
  71.6 0.0 copy-start
  71.6 1.5 fusion.60
  73.1 1.4 fusion.61
  74.6 0.7 constant_dynamic-update-slice_fusion.2
  75.3 2.6 %bitcast_reduce_fusion.3 = (f32[64,8]{1,0:T(8,128)S(1)}, f32[64,8,4096]{2,1,0:T(8,128)S(1)}) fusion(bf16[4096,1,128]{2,0,1:T(8,128)(2,1)} %get-tuple-element.119, bf16[8,64,1,8,128]{4,3,1,2,0:T(8,128)(2,1)S(1)} %get-tuple-element.118, s32[]{:T(128)} %get-tuple-element.108), kind=kOutput, calls=%fused_computation.1.clone.1 | convolution fusion | flops 541064704 | bytes 9570308 | tf_op jit(solution)/shard_map/while/body/eval_jaxpr/bjgd,njd->bjgn/dot_general | solution.py:61
  77.9 1.5 fusion.60
  79.4 1.4 fusion.61
  80.9 0.7 constant_dynamic-update-slice_fusion.2
  81.6 2.6 %bitcast_reduce_fusion.3 = (f32[64,8]{1,0:T(8,128)S(1)}, f32[64,8,4096]{2,1,0:T(8,128)S(1)}) fusion(bf16[4096,1,128]{2,0,1:T(8,128)(2,1)} %get-tuple-element.119, bf16[8,64,1,8,128]{4,3,1,2,0:T(8,128)(2,1)S(1)} %get-tuple-element.118, s32[]{:T(128)} %get-tuple-element.108), kind=kOutput, calls=%fused_computation.1.clone.1 | convolution fusion | flops 541064704 | bytes 9570308 | tf_op jit(solution)/shard_map/while/body/eval_jaxpr/bjgd,njd->bjgn/dot_general | solution.py:61
  84.2 1.5 fusion.60
  85.7 1.4 fusion.61
  87.2 0.7 constant_dynamic-update-slice_fusion.2
  87.9 2.6 %bitcast_reduce_fusion.3 = (f32[64,8]{1,0:T(8,128)S(1)}, f32[64,8,4096]{2,1,0:T(8,128)S(1)}) fusion(bf16[4096,1,128]{2,0,1:T(8,128)(2,1)} %get-tuple-element.119, bf16[8,64,1,8,128]{4,3,1,2,0:T(8,128)(2,1)S(1)} %get-tuple-element.118, s32[]{:T(128)} %get-tuple-element.108), kind=kOutput, calls=%fused_computation.1.clone.1 | convolution fusion | flops 541064704 | bytes 9570308 | tf_op jit(solution)/shard_map/while/body/eval_jaxpr/bjgd,njd->bjgn/dot_general | solution.py:61
  90.5 1.5 fusion.60
  92.0 1.4 fusion.61
  93.5 0.7 constant_dynamic-update-slice_fusion.2
  94.2 2.6 %bitcast_reduce_fusion.3 = (f32[64,8]{1,0:T(8,128)S(1)}, f32[64,8,4096]{2,1,0:T(8,128)S(1)}) fusion(bf16[4096,1,128]{2,0,1:T(8,128)(2,1)} %get-tuple-element.119, bf16[8,64,1,8,128]{4,3,1,2,0:T(8,128)(2,1)S(1)} %get-tuple-element.118, s32[]{:T(128)} %get-tuple-element.108), kind=kOutput, calls=%fused_computation.1.clone.1 | convolution fusion | flops 541064704 | bytes 9570308 | tf_op jit(solution)/shard_map/while/body/eval_jaxpr/bjgd,njd->bjgn/dot_general | solution.py:61
  96.8 1.5 fusion.60
  98.3 1.4 fusion.61
  99.8 0.7 constant_dynamic-update-slice_fusion.2
  100.6 2.6 %bitcast_reduce_fusion.3 = (f32[64,8]{1,0:T(8,128)S(1)}, f32[64,8,4096]{2,1,0:T(8,128)S(1)}) fusion(bf16[4096,1,128]{2,0,1:T(8,128)(2,1)} %get-tuple-element.119, bf16[8,64,1,8,128]{4,3,1,2,0:T(8,128)(2,1)S(1)} %get-tuple-element.118, s32[]{:T(128)} %get-tuple-element.108), kind=kOutput, calls=%fused_computation.1.clone.1 | convolution fusion | flops 541064704 | bytes 9570308 | tf_op jit(solution)/shard_map/while/body/eval_jaxpr/bjgd,njd->bjgn/dot_general | solution.py:61
  103.1 1.5 fusion.60
  104.6 1.4 fusion.61
  106.1 0.7 constant_dynamic-update-slice_fusion.2
  106.9 2.6 %bitcast_reduce_fusion.3 = (f32[64,8]{1,0:T(8,128)S(1)}, f32[64,8,4096]{2,1,0:T(8,128)S(1)}) fusion(bf16[4096,1,128]{2,0,1:T(8,128)(2,1)} %get-tuple-element.119, bf16[8,64,1,8,128]{4,3,1,2,0:T(8,128)(2,1)S(1)} %get-tuple-element.118, s32[]{:T(128)} %get-tuple-element.108), kind=kOutput, calls=%fused_computation.1.clone.1 | convolution fusion | flops 541064704 | bytes 9570308 | tf_op jit(solution)/shard_map/while/body/eval_jaxpr/bjgd,njd->bjgn/dot_general | solution.py:61
  109.5 1.5 fusion.60
  111.0 1.4 fusion.61
  112.4 0.7 constant_dynamic-update-slice_fusion.2
  113.2 2.6 %bitcast_reduce_fusion.3 = (f32[64,8]{1,0:T(8,128)S(1)}, f32[64,8,4096]{2,1,0:T(8,128)S(1)}) fusion(bf16[4096,1,128]{2,0,1:T(8,128)(2,1)} %get-tuple-element.119, bf16[8,64,1,8,128]{4,3,1,2,0:T(8,128)(2,1)S(1)} %get-tuple-element.118, s32[]{:T(128)} %get-tuple-element.108), kind=kOutput, calls=%fused_computation.1.clone.1 | convolution fusion | flops 541064704 | bytes 9570308 | tf_op jit(solution)/shard_map/while/body/eval_jaxpr/bjgd,njd->bjgn/dot_general | solution.py:61
  115.8 1.5 fusion.60
  117.3 1.4 fusion.61
  118.7 0.7 constant_dynamic-update-slice_fusion.2
  119.5 0.1 copy.30
  119.6 0.1 reshape.158
  119.8 11.8 %all_to_all.73 = f32[32,1,128]{2,1,0:T(1,128)S(1)} all-to-all(f32[32,1,128]{2,1,0:T(1,128)S(1)} %reshape.158), channel_id=1, replica_groups=mesh['prefix'=32,'req'=8] {'prefix'}, dimensions={0} | all-to-all | bytes 32768 | tf_op jit(solution)/shard_map/all_to_all | solution.py:85
  131.5 0.5 broadcast.40
  132.1 0.7 reduce.4
  132.7 0.1 reshape.159
  132.9 0.1 copy.32
  133.0 14.5 %all_to_all.74 = f32[8,2,8]{2,1,0:T(2,128)S(1)} all-to-all(f32[8,2,8]{2,1,0:T(2,128)S(1)} %bitcast.164), channel_id=1, replica_groups=mesh['prefix'=32,'req'=8] {'req'}, dimensions={0} | all-to-all | bytes 1024 | tf_op jit(solution)/shard_map/all_to_all | solution.py:95
  147.5 5.1 %all-to-all-start.1 = ((f32[32,16,1024]{2,1,0:T(8,128)}), f32[32,16,1024]{2,1,0:T(8,128)S(1)}, u32[]{:S(2)}, u32[]{:S(2)}) async-start(f32[32,16,1024]{2,1,0:T(8,128)} %bitcast.155), calls=%async_computation.1 | async-start | bytes 4194304 | tf_op jit(solution)/shard_map/all_to_all | solution.py:86
  152.7 0.1 iota_compare_fusion
  152.8 3.5 %fusion.51 = (f32[2,8,8]{2,1,0:T(8,128)S(1)}, f32[2,8,8,1024]{3,2,1,0:T(8,128)S(1)}) fusion(bf16[1,2,64,128]{3,1,2,0:T(2,128)(2,1)S(1)} %bitcast.161, pred[2,1024]{1,0:T(4,128)(4,1)S(1)} %iota_compare_fusion, bf16[2,1024,1024]{2,1,0:T(8,128)(2,1)} %param.11), kind=kOutput, calls=%fused_computation.53 | convolution fusion | flops 33947520 | bytes 4753920 | tf_op jit(solution)/shard_map/bjgd,bsjd->bjgs/dot_general | solution.py:37
  156.2 0.2 fusion.41
  156.5 0.1 add.48
  156.5 3.1 %fusion.37 = f32[1,2,64,128]{3,2,1,0:T(8,128)S(1)} fusion(f32[2,8,8,1024]{3,2,1,0:T(8,128)S(1)} %get-tuple-element.57, f32[2,8,8]{2,1,0:T(8,128)S(1)} %get-tuple-element.56, f32[2,8,8]{2,1,0:T(8,128)S(1)} %fusion.41, bf16[2,1024,1024]{2,1,0:T(8,128)(2,1)} %param.12), kind=kOutput, calls=%fused_computation.29 | convolution fusion | flops 33832960 | bytes 4785152 | tf_op jit(solution)/shard_map/bjgs,bsjd->bjgd/dot_general | solution.py:45
  159.7 0.1 copy.31
  159.9 1.9 mul.35
  161.8 2.7 %mul.36 = f32[32,16,1024]{2,1,0:T(8,128)} reshape(f32[32,16,8,128]{3,2,1,0:T(8,128)} %mul.35) | data formatting | bytes 4194304 | tf_op jit(solution)/shard_map/mul | solution.py:93
  164.5 0.1 all_to_all.66
  164.6 15.1 %all-to-all-done.1 = f32[32,16,1024]{2,1,0:T(8,128)S(1)} async-done(((f32[32,16,1024]{2,1,0:T(8,128)}), f32[32,16,1024]{2,1,0:T(8,128)S(1)}, u32[]{:S(2)}, u32[]{:S(2)}) %all-to-all-start.1) | async-done | bytes 2097184 | tf_op jit(solution)/shard_map/all_to_all | solution.py:86
  179.7 1.8 multiply_reduce_fusion
  181.6 0.7 all_to_all.60
  182.2 3.4 %all-to-all-start.3 = ((f32[8,2,1024]{2,1,0:T(2,128)}), f32[8,2,1024]{2,1,0:T(2,128)S(1)}, u32[]{:S(2)}, u32[]{:S(2)}) async-start(f32[8,2,1024]{2,1,0:T(2,128)} %all_to_all.60), calls=%async_computation.3 | async-start | bytes 131072 | tf_op jit(solution)/shard_map/all_to_all | solution.py:96
  185.6 0.1 broadcast_bitcast_fusion
  185.7 8.2 %all-to-all-done.3 = f32[8,2,1024]{2,1,0:T(2,128)S(1)} async-done(((f32[8,2,1024]{2,1,0:T(2,128)}), f32[8,2,1024]{2,1,0:T(2,128)S(1)}, u32[]{:S(2)}, u32[]{:S(2)}) %all-to-all-start.3) | async-done | bytes 65568 | tf_op jit(solution)/shard_map/all_to_all | solution.py:96
  193.9 0.8 fusion.44
  (45 shorter events, 0.7 us)
Async XLA Ops:
  6.5 61.0 %all-gather.2.cloned.1.call-start = ((), (), s32[]{:S(2)}) async-start(), calls=%async_computation.5 | async-start | bytes 1081344 | tf_op jit(solution)/shard_map/all_gather | solution.py:30
  71.6 1.5 copy-start
  77.9 1.5 copy-start
  84.2 1.5 copy-start
  90.5 1.5 copy-start
  96.8 1.5 copy-start
  103.1 1.5 copy-start
  109.4 1.5 copy-start
  115.7 1.5 copy-start
  119.5 33.2 %copy-start.2 = (s32[2]{0:T(128)S(1)}, s32[2]{0:T(128)}, u32[]{:S(2)}) copy-start(s32[2]{0:T(128)} %param.13) | copy-start | bytes 28
  119.5 33.3 %copy-start.1 = (bf16[2,8192]{1,0:T(2,128)(2,1)S(1)}, bf16[2,8192]{1,0:T(2,128)(2,1)}, u32[]{:S(2)}) copy-start(bf16[2,8192]{1,0:T(2,128)(2,1)} %param.8) | copy-start | bytes 98308
  147.5 32.2 %all-to-all-start.1 = ((f32[32,16,1024]{2,1,0:T(8,128)}), f32[32,16,1024]{2,1,0:T(8,128)S(1)}, u32[]{:S(2)}, u32[]{:S(2)}) async-start(f32[32,16,1024]{2,1,0:T(8,128)} %bitcast.155), calls=%async_computation.1 | async-start | bytes 4194304 | tf_op jit(solution)/shard_map/all_to_all | solution.py:86
  182.2 11.7 %all-to-all-start.3 = ((f32[8,2,1024]{2,1,0:T(2,128)}), f32[8,2,1024]{2,1,0:T(2,128)S(1)}, u32[]{:S(2)}, u32[]{:S(2)}) async-start(f32[8,2,1024]{2,1,0:T(2,128)} %all_to_all.60), calls=%async_computation.3 | async-start | bytes 131072 | tf_op jit(solution)/shard_map/all_to_all | solution.py:96
Sparse Core Ops, SparseCore 0:
  23.8 43.6 all-gather.1
where the time goes:
time: 204 us; the launch traced here: 202 us
  waiting for transfers between devices  67.2 us (33%)
  blocking collectives  42.8 us (21%)
  matrix products  38.3 us (19%)
  other arithmetic  15.8 us (8%)
  local copies, waits for them, and re-layouts  15 us (7%)
  between operations  13.5 us (7%)
  starting transfers between devices  8.48 us (4%)
    all_gather x1, waiting for transfers between devices, local(): gathered = lax.all_gather(routed, 'prefix', axis=0, tiled=True)  43.8 us
    dot_general x8, matrix products, prefix_block(): jnp.einsum('bjgd,njd->bjgn', query_block, keys_local, preferred_element_t...  20.5 us
    all_to_all x1, blocking collectives, local(): lax.all_to_all(queries, 'req', split_axis=1, concat_axis=0, tiled=True)  16.5 us
    all_to_all x1, waiting for transfers between devices, local(): lax.all_to_all(partial_out, 'prefix', split_axis=0, concat_axis=0, tiled=...  15.1 us
    all_to_all x1, blocking collectives, local(): lax.all_to_all(mine_mass, 'req', split_axis=0, concat_axis=1, tiled=True)  14.5 us
    reduce_sum x8, other arithmetic, prefix_block(): block_total = jnp.sum(weights, axis=-1)  12 us
    all_to_all x1, blocking collectives, local(): lax.all_to_all(log_mass, 'prefix', split_axis=0, concat_axis=0, tiled=True)  11.8 us
    dot_general x8, matrix products, prefix_block(): jnp.einsum('bjgn,njd->bjgd', weights.astype(jnp.bfloat16), values_local,...  11.3 us
  transfers between devices with their start and end apart: 3, of which 3 were waited for; matrix products, arithmetic and copies ran while one was open for 6% of the time, Pallas kernels for 0%

commit v1 on v0

v1 whole, which is shorter than its diff:
```python
import functools
import math

import jax
import jax.numpy as jnp
from jax import lax
from jax.experimental import pallas as pl
from jax.experimental.pallas import tpu as pltpu
from jax.sharding import PartitionSpec as P

HEADS = 64
KVH = 8
HD = 128
GROUP = HEADS // KVH
SIDE = 4
CHIPS = SIDE * SIDE
ZS = 8
CHUNK = 1024
MESH = pl.DeviceIdType.MESH
F32 = jnp.float32
BF16 = jnp.bfloat16
LOG2_SCALE = math.log2(math.e) / math.sqrt(HD)
LOW = -1e30


def hop(a):
    return jnp.where(a == 0, 2, jnp.where(a == 1, 1, jnp.where(a == 2, 3, 0)))


def kernel(
    q_ref, k_hbm, v_hbm, sk_hbm, sv_hbm, len_ref, out_ref,
    kbuf, vbuf, vt, s0, s1, sk, sv, qf, qz, qt, osend, oland, zsend, zland, sfx_o, sfx_b,
    load_sem, sib_send, sib_recv, z1_send, z1_recv, q_send, q_recv, o_send, o_recv, z2_send, z2_recv,
):
    p = lax.axis_index("prefix")
    z = lax.axis_index("req")
    chip = p // 2
    core = p % 2
    cx = chip // SIDE
    cy = chip % SIDE
    sibling = p + 1 - 2 * core
    keys = k_hbm.shape[0]
    rows = 2 * CHIPS * 8

    def chip_at(t):
        return ((cx + hop(t // SIDE)) % SIDE) * SIDE + (cy + hop(t % SIDE)) % SIDE

    def load(src, dst, i):
        copy = pltpu.make_async_copy(src, dst, load_sem.at[i])
        copy.start()
        return copy

    load_v = load(v_hbm, vbuf, 0)
    load_k = load(k_hbm, kbuf.at[0], 1)
    loads = []
    for r in range(2):
        loads.append((load(sk_hbm.at[r], sk.at[r], 2 + 2 * r), load(sv_hbm.at[r], sv.at[r], 3 + 2 * r)))

    barrier = pltpu.get_barrier_semaphore()
    for d in range(1, ZS):
        pl.semaphore_signal(barrier, inc=1, device_id=(p, (z + d) % ZS), device_id_type=MESH)
    for t in range(CHIPS - 1):
        pl.semaphore_signal(barrier, inc=1, device_id=(2 * chip_at(t) + core, z), device_id_type=MESH)
    pl.semaphore_signal(barrier, inc=1, device_id=(sibling, z), device_id_type=MESH)

    own_q = q_ref[...].astype(F32)
    for g in range(KVH):
        for h in range(GROUP):
            at = (g * GROUP + h) * HD
            for r in range(2):
                qf[g, r, h : h + 1, :] = own_q[r : r + 1, at : at + HD]

    pl.semaphore_wait(barrier, ZS - 1 + CHIPS - 1 + 1)

    def z1_copy(other):
        return pltpu.make_async_remote_copy(
            src_ref=qf.at[other], dst_ref=qz.at[z],
            send_sem=z1_send.at[other], recv_sem=z1_recv.at[z],
            device_id=(p, other), device_id_type=MESH,
        )

    def z1_arrival(other):
        return pltpu.make_async_remote_copy(
            src_ref=qf.at[other], dst_ref=qz.at[other],
            send_sem=z1_send.at[other], recv_sem=z1_recv.at[other],
            device_id=(p, other), device_id_type=MESH,
        )

    for d in range(1, ZS):
        z1_copy((z + d) % ZS).start()
    qz[z] = qf[z]

    sib_k = pltpu.make_async_remote_copy(
        src_ref=k_hbm, dst_ref=kbuf.at[1],
        send_sem=sib_send.at[0], recv_sem=sib_recv.at[0],
        device_id=(sibling, z), device_id_type=MESH,
    )
    sib_k.start()
    load_v.wait()
    for c in range(keys // CHUNK):
        part = vbuf[c * CHUNK : (c + 1) * CHUNK, :].astype(F32)
        vt[0, :, c * CHUNK : (c + 1) * CHUNK] = part.T.astype(BF16)
    sib_v = pltpu.make_async_remote_copy(
        src_ref=vt.at[0], dst_ref=vt.at[1],
        send_sem=sib_send.at[1], recv_sem=sib_recv.at[1],
        device_id=(sibling, z), device_id_type=MESH,
    )
    sib_v.start()

    for d in range(1, ZS):
        z1_arrival((z + d) % ZS).wait_recv()
    qt[chip] = qz[...].reshape(2 * ZS * GROUP, HD).T.astype(BF16)

    def q_copy(t):
        return pltpu.make_async_remote_copy(
            src_ref=qt.at[chip], dst_ref=qt.at[chip],
            send_sem=q_send.at[t], recv_sem=q_recv.at[chip],
            device_id=(2 * chip_at(t) + core, z), device_id_type=MESH,
        )

    def q_arrival(t):
        c = chip_at(t)
        return pltpu.make_async_remote_copy(
            src_ref=qt.at[c], dst_ref=qt.at[c],
            send_sem=q_send.at[t], recv_sem=q_recv.at[c],
            device_id=(2 * c + core, z), device_id_type=MESH,
        )

    for t in range(CHIPS - 1):
        q_copy(t).start()

    for r in range(2):
        loads[r][0].wait()
        loads[r][1].wait()
        live = lax.broadcasted_iota(jnp.int32, (GROUP, sk.shape[1]), 1) < len_ref[r]
        for g in range(KVH):
            q8 = qf[g, r].astype(BF16)
            s = lax.dot_general(
                q8, sk[r, :, g * HD : (g + 1) * HD], (((1,), (1,)), ((), ())),
                preferred_element_type=F32,
            )
            s = jnp.where(live, s * LOG2_SCALE, LOW)
            top = jnp.max(s, axis=1, keepdims=True)
            w = jnp.exp2(s - top)
            total = jnp.sum(w, axis=1, keepdims=True)
            o = jnp.dot(w.astype(BF16), sv[r, :, g * HD : (g + 1) * HD], preferred_element_type=F32)
            sfx_o[g, r] = o / total
            sfx_b[g, r] = jnp.broadcast_to(top + jnp.log2(total), (GROUP, HD))

    load_k.wait()
    sib_k.wait_recv()
    sib_v.wait_recv()
    per_half = keys // CHUNK

    def split_queries(i):
        parts = [qt[chip_at(2 * i + u)] for u in range(2)]
        both = jnp.concatenate(parts, axis=1).astype(F32) * LOG2_SCALE
        high = both.astype(BF16)
        low = (both - high.astype(F32)).astype(BF16)
        return jnp.concatenate([high, low], axis=0)

    def o_copy(t):
        return pltpu.make_async_remote_copy(
            src_ref=osend.at[t], dst_ref=oland.at[chip],
            send_sem=o_send.at[t], recv_sem=o_recv.at[chip],
            device_id=(2 * chip_at(t) + core, z), device_id_type=MESH,
        )

    def o_arrival(t):
        c = chip_at(t)
        return pltpu.make_async_remote_copy(
            src_ref=osend.at[t], dst_ref=oland.at[c],
            send_sem=o_send.at[t], recv_sem=o_recv.at[c],
            device_id=(2 * c + core, z), device_id_type=MESH,
        )

    def step(now, later, i, top):
        if later is not None:
            for u in range(2):
                if not (isinstance(i, int) and 2 * (i + 1) + u == CHIPS - 1):
                    q_arrival(2 * (i + 1) + u).wait_recv()
            queries = split_queries(i + 1)
            new_top = jnp.full((8, rows), LOW, F32)
        if now is not None:
            acc = jnp.zeros((HD, rows), F32)
            total = jnp.zeros((8, rows), F32)
        for c in range(2 * per_half):
            half, at = c // per_half, (c % per_half) * CHUNK
            here = slice(c * CHUNK, (c + 1) * CHUNK)
            if later is not None:
                k = kbuf[half, at : at + CHUNK, :]
                s = jnp.dot(jnp.concatenate([k, k], axis=1), queries, preferred_element_type=F32)
                later[here, :] = s
                new_top = jnp.maximum(new_top, s.reshape(CHUNK // 8, 8, rows).max(axis=0))
            if now is not None:
                w = jnp.exp2(now[here, :] - top)
                total = total + w.reshape(CHUNK // 8, 8, rows).sum(axis=0)
                acc = acc + jnp.dot(vt[half, :, at : at + CHUNK], w.astype(BF16), preferred_element_type=F32)
        if now is not None:
            mass = jnp.broadcast_to(total.sum(axis=0, keepdims=True), (4, rows))
            mass = jnp.concatenate([mass, jnp.broadcast_to(top, (4, rows))], axis=0)
            for u in range(2):
                t = 2 * i + u
                cols = slice(u * rows // 2, (u + 1) * rows // 2)
                osend[t, :HD, :] = acc[:, cols]
                osend[t, HD:, :] = mass[:, cols]
                if not (isinstance(i, int) and t == CHIPS - 1):
                    o_copy(t).start()
        if later is not None:
            return new_top.max(axis=0, keepdims=True)

    pairs = CHIPS // 2
    top = step(None, s0, -1, None)

    def two_steps(j, top):
        top = step(s0, s1, 2 * j, top)
        return step(s1, s0, 2 * j + 1, top)

    top = lax.fori_loop(0, pairs // 2 - 1, two_steps, top)
    top = step(s0, s1, pairs - 2, top)
    step(s1, None, pairs - 1, top)

    for t in range(CHIPS - 1):
        o_arrival(t).wait_recv()
    tops = [oland[chip_at(t), HD + 4 : HD + 5, :] for t in range(CHIPS - 1)]
    tops.append(osend[CHIPS - 1, HD + 4 : HD + 5, :])
    top = functools.reduce(jnp.maximum, tops)
    acc = jnp.zeros((HD, rows // 2), F32)
    total = jnp.zeros((1, rows // 2), F32)
    for t in range(CHIPS):
        part = osend.at[t] if t == CHIPS - 1 else oland.at[chip_at(t)]
        share = jnp.exp2(tops[t] - top)
        acc = acc + part[:HD, :] * share
        total = total + part[HD : HD + 1, :] * share
    zsend[:, 0] = (acc / total).T.reshape(ZS, 2 * GROUP, HD)
    zsend[:, 1] = jnp.broadcast_to(top + jnp.log2(total), (HD, rows // 2)).T.reshape(ZS, 2 * GROUP, HD)

    def z2_copy(other):
        return pltpu.make_async_remote_copy(
            src_ref=zsend.at[other], dst_ref=zland.at[z],
            send_sem=z2_send.at[other], recv_sem=z2_recv.at[z],
            device_id=(p, other), device_id_type=MESH,
        )

    def z2_arrival(other):
        return pltpu.make_async_remote_copy(
            src_ref=zsend.at[other], dst_ref=zland.at[other],
            send_sem=z2_send.at[other], recv_sem=z2_recv.at[other],
            device_id=(p, other), device_id_type=MESH,
        )

    for d in range(1, ZS):
        z2_copy((z + d) % ZS).start()
    zland[z] = zsend[z]
    for d in range(1, ZS):
        z2_arrival((z + d) % ZS).wait_recv()
    for g in range(KVH):
        o = zland[g, 0].reshape(2, GROUP, HD)
        b = zland[g, 1].reshape(2, GROUP, HD)
        share = 1.0 / (1.0 + jnp.exp2(sfx_b[g] - b))
        out_ref[:, g] = o * share + sfx_o[g] * (1.0 - share)

    for d in range(1, ZS):
        z1_copy((z + d) % ZS).wait_send()
        z2_copy((z + d) % ZS).wait_send()
    for t in range(CHIPS - 1):
        q_copy(t).wait_send()
        o_copy(t).wait_send()
    sib_k.wait_send()
    sib_v.wait_send()


def local(queries, prefix_keys, prefix_values, suffix_keys, suffix_values, suffix_lengths):
    keys = prefix_keys.shape[0]
    positions = suffix_keys.shape[1]
    rows = 2 * CHIPS * 8
    dma = pltpu.SemaphoreType.DMA
    hbm = pl.BlockSpec(memory_space=pl.ANY)
    out = pl.pallas_call(
        kernel,
        out_shape=jax.ShapeDtypeStruct((2, KVH, GROUP, HD), F32),
        in_specs=[
            pl.BlockSpec(memory_space=pltpu.VMEM), hbm, hbm, hbm, hbm,
            pl.BlockSpec(memory_space=pltpu.SMEM),
        ],
        out_specs=pl.BlockSpec(memory_space=pltpu.VMEM),
        scratch_shapes=[
            pltpu.VMEM((2, keys, HD), BF16),
            pltpu.VMEM((keys, HD), BF16),
            pltpu.VMEM((2, HD, keys), BF16),
            pltpu.VMEM((2 * keys, rows), F32),
            pltpu.VMEM((2 * keys, rows), F32),
            pltpu.VMEM((2, positions, KVH * HD), BF16),
            pltpu.VMEM((2, positions, KVH * HD), BF16),
            pltpu.VMEM((KVH, 2, GROUP, HD), F32),
            pltpu.VMEM((ZS, 2, GROUP, HD), F32),
            pltpu.VMEM((CHIPS, HD, rows // 2), BF16),
            pltpu.VMEM((CHIPS, HD + 8, rows // 2), F32),
            pltpu.VMEM((CHIPS, HD + 8, rows // 2), F32),
            pltpu.VMEM((ZS, 2, 2 * GROUP, HD), F32),
            pltpu.VMEM((KVH, 2, 2 * GROUP, HD), F32),
            pltpu.VMEM((KVH, 2, GROUP, HD), F32),
            pltpu.VMEM((KVH, 2, GROUP, HD), F32),
            dma((6,)),
            dma((2,)), dma((2,)),
            dma((ZS,)), dma((ZS,)),
            dma((CHIPS,)), dma((CHIPS,)),
            dma((CHIPS,)), dma((CHIPS,)),
            dma((ZS,)), dma((ZS,)),
        ],
        compiler_params=pltpu.CompilerParams(
            collective_id=0, has_side_effects=True, vmem_limit_bytes=56 * 2**20
        ),
        name="attend",
    )(queries, prefix_keys, prefix_values, suffix_keys, suffix_values, suffix_lengths)
    return out.reshape(2, HEADS * HD)


def solution(mesh):
    return jax.shard_map(
        local,
        mesh=mesh,
        in_specs=(
            P(("prefix", "req"), None),
            P("prefix", "req"),
            P("prefix", "req"),
            P(("prefix", "req"), None, None),
            P(("prefix", "req"), None, None),
            P(("prefix", "req")),
        ),
        out_specs=P(("prefix", "req"), None),
        check_vma=False,
    )
```

time: 204 us -> 50.1 us (0.25); the launches traced: 202 us -> 49.9 us
  waiting for transfers between devices: 67.2 us -> 0 us
  Pallas kernels: 0 us -> 48.4 us
  blocking collectives: 42.8 us -> 0 us
  matrix products: 38.3 us -> 0 us
  other arithmetic: 15.8 us -> 0 us
  between operations: 13.5 us -> 0.01 us
  local copies, waits for them, and re-layouts: 15 us -> 1.52 us
  starting transfers between devices: 8.48 us -> 0 us
    pallas_call x0 -> x1, Pallas kernels: none -> 48.4 us  [local(): pl.pallas_call(kernel, out_shape=jax.ShapeDtypeStruct((2, KVH, GROUP, HD)...]
    all_gather x1 -> x0, waiting for transfers between devices: 43.8 us -> none  [local(): gathered = lax.all_gather(routed, 'prefix', axis=0, tiled=True)]
    all_to_all x3 -> x0, blocking collectives: 42.8 us -> none  [the longest x1 16.5 us: local(): lax.all_to_all(queries, 'req', split_axis=1, concat_axis=0, tiled=True)]
    dot_general x18 -> x0, matrix products: 38.3 us -> none  [the longest x8 20.5 us: prefix_block(): jnp.einsum('bjgd,njd->bjgn', query_block, keys_local, preferred_element_t...]
    all_to_all x2 -> x0, waiting for transfers between devices: 23.3 us -> none  [the longest x1 15.1 us: local(): lax.all_to_all(partial_out, 'prefix', split_axis=0, concat_axis=0, tiled=...]
    reduce_sum x11 -> x0, other arithmetic: 14.1 us -> none  [the longest x8 12 us: prefix_block(): block_total = jnp.sum(weights, axis=-1)]
    all_to_all x2 -> x0, starting transfers between devices: 8.47 us -> none  [the longest x1 5.12 us: local(): lax.all_to_all(partial_out, 'prefix', split_axis=0, concat_axis=0, tiled=...]
    dynamic_update_slice x8 -> x0, local copies, waits for them, and re-layouts: 5.85 us -> none  [local(): log_mass, partial_out = lax.map(prefix_block, query_blocks)]
  transfers between devices with their start and end apart: 3 -> 0, of which waited for: 3 -> 0; matrix products, arithmetic and copies ran while one was open for 6% -> 0% of each run, Pallas kernels for 0% -> 0%
where the time goes in v1:
time: 50.1 us; the launch traced here: 49.9 us
  Pallas kernels  48.4 us (97%)
  local copies, waits for them, and re-layouts  1.52 us (3%)
    pallas_call x1, Pallas kernels, local(): pl.pallas_call(kernel, out_shape=jax.ShapeDtypeStruct((2, KVH, GROUP, HD)...  48.4 us
    unnamed x1, local copies, waits for them, and re-layouts  1.52 us

profile of v1, /device:TPU:8, one launch (start us, length us, event | category | flops | bytes accessed | tf_op | source)
XLA Modules:
  0.0 49.9 jit_solution(7787203279062722070)
XLA Ops:
  0.0 48.4 %attend.1 = f32[2,8,8,128]{3,2,1,0:T(8,128)} custom-call(bf16[2,8192]{1,0:T(2,128)(2,1)} %q_ref.1, bf16[4096,128]{1,0:T(8,128)(2,1)} %k_hbm.1, bf16[4096,128]{1,0:T(8,128)(2,1)} %v_hbm.1, bf16[2,1024,1024]{2,1,0:T(8,128)(2,1)} %sk_hbm.1, bf16[2,1024,1024]{2,1,0:T(8,128)(2,1)} %sv_hbm.1, s32[2]{0:T(128)} %len_ref.1), custom_call_target="tpu_custom_call" | custom-call | tf_op jit(solution)/shard_map/attend/pallas_call | solution.py:279
  48.4 1.5 %copy.9 = f32[1,2,64,128]{3,1,2,0:T(2,128)} copy(f32[1,2,64,128]{3,2,1,0:T(8,128)} %bitcast.5) | data formatting | bytes 131072
